TPU v7x, 256 devices: a whole 4x4x8 slice. The times are simulated.
256 devices in a mesh: dom: 32 (over y, x, core), blk: 8 (over z).
Axes of the slice: x: 4, y: 4, z: 8, core: 2. Of those that a mesh axis runs over, the one named last changes fastest.
Arguments:
- source: bfloat16 [4096, 192], P(('dom', 'blk')), may hold values from -6 to 6
- lam_init: bfloat16 [4096, 192], P(('dom', 'blk')), may hold values from -6 to 6
- offd: bfloat16 [4096, 192, 1152], P(('dom', 'blk')), may hold values from -0.1875 to 0.1875
- dinv: bfloat16 [192, 786432], P(None, ('dom', 'blk')), may hold values from -0.4375 to 0.4375
- colidx: int32 [4096, 6], P(('dom', 'blk')), may hold values from 0 to 191
- face_list: int32 [32, 64], P('dom'), may hold values from 0 to 127
- partner: int32 [32], P('dom'), may hold values from 0 to 31, as said below
- perf_block: int32 [32768], P(('dom', 'blk')), may hold values from 0 to 15
- perf_well: int32 [32768], P(('dom', 'blk')), may hold values from 0 to 63
- perf_sens: bfloat16 [32768, 192], P(('dom', 'blk')), may hold values from -0.21875 to 0.21875
- obj_weight: float32 [1024], replicated, may hold values from 0.5 to 2
- step_index: int32 [1], replicated, may hold values from 0 to 1023
Outputs:
- adjoint: float32 [4096, 192], P(('dom', 'blk'))
- control_grad: float32 [2048], P(('dom', 'blk'))
Inputs may be any that keep to these rules, and one draw needn't show every extreme that they name: Below 128 an own block of the partition, from 128 on halo block colidx - 128. `face_list`: blocks of the partition's own 128, repeats possible. A pairing: partner[p] != p and partner[partner[p]] == p.
All inputs are finite; a program needn't handle non-finite values.
Results may differ from a plain program's by a relative error of at most 0.0054.
Values may be sent and summed in bfloat16 or wider, within the bound.
No kernel may reach another device: no remote copies, remote signals or barrier semaphores. Data moves between devices by JAX's collectives and lax.ppermute only.
A program may use at most 64 MiB of HBM per device.

v0:
```python
import jax
import jax.numpy as jnp
from jax import lax
from jax.sharding import PartitionSpec as P

WP = 64


def cross_partition(face_rows, partner_id):
    slot_count = lax.axis_size("dom")
    onehot = (jnp.arange(slot_count, dtype=jnp.int32) == partner_id).astype(jnp.bfloat16)
    outgoing = onehot[:, None, None] * face_rows[None, :, :]
    incoming = lax.all_to_all(outgoing, "dom", split_axis=0, concat_axis=0, tiled=True)
    halo_blocks = lax.dynamic_index_in_dim(incoming, partner_id, 0, keepdims=False)
    return halo_blocks


def extended_state(state, face_index, partner_id):
    partition = lax.all_gather(state, "blk", axis=0, tiled=True)
    halo_blocks = cross_partition(partition[face_index], partner_id)
    return jnp.concatenate([partition, halo_blocks], axis=0)


def sweep_once(state, forcing, offd, inverses, colidx, face_index, partner_id):
    extended = extended_state(state, face_index, partner_id)
    picked = extended[colidx].reshape(colidx.shape[0], -1)
    coupled = jnp.einsum("bim,bm->bi", offd, picked, preferred_element_type=jnp.float32)
    residual_rhs = (forcing - coupled).astype(jnp.bfloat16)
    return jnp.einsum("ibj,bj->bi", inverses, residual_rhs, preferred_element_type=jnp.float32)


def body(
    source,
    lam_init,
    offd,
    dinv,
    colidx,
    face_list,
    partner,
    perf_block,
    perf_well,
    perf_sens,
    obj_weight,
    step_index,
):
    weight = lax.dynamic_index_in_dim(obj_weight, step_index[0], 0, keepdims=False)
    forcing = weight * source.astype(jnp.float32)
    width = source.shape[1]
    inverses = dinv.reshape(width, source.shape[0], width)
    face_index = face_list[0]
    partner_id = partner[0]
    first_pass = sweep_once(
        lam_init, forcing, offd, inverses, colidx, face_index, partner_id
    ).astype(jnp.bfloat16)
    adjoint = sweep_once(first_pass, forcing, offd, inverses, colidx, face_index, partner_id)
    contrib = jnp.sum(perf_sens.astype(jnp.float32) * adjoint[perf_block], axis=1)
    onehot = (perf_well[:, None] == jnp.arange(WP, dtype=jnp.int32)[None, :]).astype(jnp.float32)
    well_terms = -jnp.dot(contrib, onehot, precision=lax.Precision.HIGHEST)
    control_grad = lax.psum_scatter(well_terms, "blk", scatter_dimension=0, tiled=True)
    return (adjoint, control_grad)


def solution(mesh):
    placed = (
        P(("dom", "blk"), None),
        P(("dom", "blk"), None),
        P(("dom", "blk"), None, None),
        P(None, ("dom", "blk")),
        P(("dom", "blk"), None),
        P("dom", None),
        P("dom"),
        P(("dom", "blk")),
        P(("dom", "blk")),
        P(("dom", "blk"), None),
        P(),
        P(),
    )
    return jax.shard_map(
        body,
        mesh=mesh,
        in_specs=placed,
        out_specs=(P(("dom", "blk"), None), P(("dom", "blk"))),
        check_vma=False,
    )
```

profile of v0, /device:TPU:2, one launch (start us, length us, event | category | flops | bytes accessed | tf_op | source)
XLA Modules:
  0.0 136.8 jit_solution(17076358415785166185)
XLA Ops:
  1.3 28.4 %all_gather.6 = bf16[128,192]{1,0:T(8,128)(2,1)S(1)} all-gather(bf16[16,192]{1,0:T(8,128)(2,1)} %param.13), channel_id=1, replica_groups=mesh['dom'=32,'blk'=8] {'blk'}, dimensions={0}, use_global_device_ids=true | all-gather | bytes 55296 | tf_op jit(solution)/shard_map/all_gather | solution.py:19
  29.7 0.7 fusion.10
  30.3 0.7 gather_fusion
  31.0 0.0 copy-start.4
  31.1 0.0 copy-start.1
  31.1 1.2 broadcast_multiply_fusion.1
  32.2 7.7 %all-to-all-start = ((bf16[32,64,192]{2,1,0:T(8,128)(2,1)}), bf16[32,64,192]{2,1,0:T(8,128)(2,1)}, u32[]{:S(2)}, u32[]{:S(2)}) async-start(bf16[32,64,192]{2,1,0:T(8,128)(2,1)} %broadcast_multiply_fusion.1), calls=%async_computation | async-start | bytes 2097152 | tf_op jit(solution)/shard_map/all_to_all | solution.py:13
  39.9 0.0 copy-done.4
  40.0 0.1 copy.18
  40.0 0.1 reshape.62
  40.8 0.0 copy-done.1
  40.8 0.7 copy.29
  41.5 1.3 dynamic_slice.11
  42.8 13.3 %all-to-all-done = bf16[32,64,192]{2,1,0:T(8,128)(2,1)} async-done(((bf16[32,64,192]{2,1,0:T(8,128)(2,1)}), bf16[32,64,192]{2,1,0:T(8,128)(2,1)}, u32[]{:S(2)}, u32[]{:S(2)}) %all-to-all-start) | async-done | bytes 786464 | tf_op jit(solution)/shard_map/all_to_all | solution.py:13
  56.1 0.8 dynamic-slice_bitcast_fusion.1
  56.9 0.8 gather_fusion.1
  57.7 0.1 reshape.110
  57.8 0.0 copy-start.3
  57.8 5.2 %fusion.12 = f32[16,1,192]{2,1,0:T(1,128)S(1)} fusion(bf16[16,1152,1]{1,2,0:T(2,128)(2,1)S(1)} %reshape.110, bf16[16,192,1152]{2,1,0:T(8,128)(2,1)} %param.14), kind=kOutput, calls=%fused_computation.38 | convolution fusion | flops 7077888 | bytes 7127040 | tf_op jit(solution)/shard_map/bim,bm->bi/dot_general | solution.py:27
  62.9 0.0 copy-done.3
  62.9 0.7 fusion.8
  63.6 0.3 fusion.6
  63.9 24.6 %all_gather.7 = bf16[128,192]{1,0:T(8,128)(2,1)S(1)} all-gather(bf16[16,192]{1,0:T(8,128)(2,1)S(1)} %bitcast.59), channel_id=1, replica_groups=mesh['dom'=32,'blk'=8] {'blk'}, dimensions={0}, use_global_device_ids=true | all-gather | bytes 55296 | tf_op jit(solution)/shard_map/all_gather | solution.py:19
  88.5 0.7 gather_fusion.2
  89.2 0.0 copy-start.2
  89.2 0.0 copy-start.7
  89.2 0.0 copy-start.5
  89.2 1.1 broadcast_multiply_fusion
  90.3 5.0 %all-to-all-start.1 = ((bf16[32,64,192]{2,1,0:T(8,128)(2,1)}), bf16[32,64,192]{2,1,0:T(8,128)(2,1)S(1)}, u32[]{:S(2)}, u32[]{:S(2)}) async-start(bf16[32,64,192]{2,1,0:T(8,128)(2,1)} %broadcast_multiply_fusion), calls=%async_computation.1 | async-start | bytes 2097152 | tf_op jit(solution)/shard_map/all_to_all | solution.py:13
  95.4 0.0 copy-done.2
  95.4 0.1 copy.19
  95.5 0.0 copy-done.7
  95.5 0.6 dynamic-slice
  96.8 0.0 copy-done.5
  96.8 14.8 %all-to-all-done.1 = bf16[32,64,192]{2,1,0:T(8,128)(2,1)S(1)} async-done(((bf16[32,64,192]{2,1,0:T(8,128)(2,1)}), bf16[32,64,192]{2,1,0:T(8,128)(2,1)S(1)}, u32[]{:S(2)}, u32[]{:S(2)}) %all-to-all-start.1) | async-done | bytes 786464 | tf_op jit(solution)/shard_map/all_to_all | solution.py:13
  111.6 0.8 gather_fusion.3
  112.4 0.1 reshape.112
  112.5 5.2 %fusion.13 = f32[16,1,192]{2,1,0:T(1,128)S(1)} fusion(bf16[16,1152,1]{1,2,0:T(2,128)(2,1)S(1)} %reshape.112, bf16[16,192,1152]{2,1,0:T(8,128)(2,1)} %param.14), kind=kOutput, calls=%fused_computation.39 | convolution fusion | flops 7077888 | bytes 7127040 | tf_op jit(solution)/shard_map/bim,bm->bi/dot_general | solution.py:27
  117.7 0.0 copy-start.6
  117.7 0.7 fusion.9
  118.4 0.3 fusion.4
  118.7 0.8 gather_fusion.4
  119.5 0.1 multiply_reduce_fusion
  119.6 0.0 copy-done.6
  119.6 0.2 fusion
  119.8 16.4 %all-reduce = f32[64]{0:T(128)S(1)} all-reduce(f32[64]{0:T(128)S(1)} %fusion), channel_id=2, replica_groups=mesh['dom'=32,'blk'=8] {'blk'}, use_global_device_ids=true, to_apply=%region_1.2.clone | all-reduce | flops 64 | bytes 512
  136.2 0.6 dynamic-slice.1
  136.8 0.0 copy-done
  (12 shorter events, 0.1 us)
Async XLA Ops:
  31.0 8.9 %copy-start.4 = (s32[16,6]{0,1:T(8,128)S(1)}, s32[16,6]{0,1:T(8,128)}, u32[]{:S(2)}) copy-start(s32[16,6]{0,1:T(8,128)} %param.16) | copy-start | bytes 1156
  31.1 9.7 %copy-start.1 = (bf16[192,3072]{1,0:T(8,128)(2,1)S(1)}, bf16[192,3072]{1,0:T(8,128)(2,1)}, u32[]{:S(2)}) copy-start(bf16[192,3072]{1,0:T(8,128)(2,1)} %param.15) | copy-start | bytes 3538948
  32.2 23.8 %all-to-all-start = ((bf16[32,64,192]{2,1,0:T(8,128)(2,1)}), bf16[32,64,192]{2,1,0:T(8,128)(2,1)}, u32[]{:S(2)}, u32[]{:S(2)}) async-start(bf16[32,64,192]{2,1,0:T(8,128)(2,1)} %broadcast_multiply_fusion.1), calls=%async_computation | async-start | bytes 2097152 | tf_op jit(solution)/shard_map/all_to_all | solution.py:13
  57.8 5.2 %copy-start.3 = (bf16[16,192]{1,0:T(8,128)(2,1)S(1)}, bf16[16,192]{1,0:T(8,128)(2,1)}, u32[]{:S(2)}) copy-start(bf16[16,192]{1,0:T(8,128)(2,1)} %param.12) | copy-start | bytes 18436
  89.2 6.2 %copy-start.2 = (bf16[128,192]{0,1:T(8,128)(2,1)S(1)}, bf16[128,192]{0,1:T(8,128)(2,1)}, u32[]{:S(2)}) copy-start(bf16[128,192]{0,1:T(8,128)(2,1)} %param.21) | copy-start | bytes 147460
  89.2 6.3 %copy-start.7 = (u32[256]{0:T(256)S(1)}, u32[256]{0:T(256)}, u32[]{:S(2)}) copy-start(u32[256]{0:T(256)} %constant.35) | copy-start | bytes 3076
  89.2 7.6 %copy-start.5 = (s32[128]{0:T(128)S(1)}, s32[128]{0:T(128)}, u32[]{:S(2)}) copy-start(s32[128]{0:T(128)} %param.19) | copy-start | bytes 1540
  90.3 21.3 %all-to-all-start.1 = ((bf16[32,64,192]{2,1,0:T(8,128)(2,1)}), bf16[32,64,192]{2,1,0:T(8,128)(2,1)S(1)}, u32[]{:S(2)}, u32[]{:S(2)}) async-start(bf16[32,64,192]{2,1,0:T(8,128)(2,1)} %broadcast_multiply_fusion), calls=%async_computation.1 | async-start | bytes 2097152 | tf_op jit(solution)/shard_map/all_to_all | solution.py:13
  117.7 1.9 %copy-start.6 = (s32[128]{0:T(128)S(1)}, s32[128]{0:T(128)}, u32[]{:S(2)}) copy-start(s32[128]{0:T(128)} %param.20) | copy-start | bytes 1540
  118.7 18.1 %copy-start = (f32[16,1,192]{2,0,1:T(8,128)}, f32[16,1,192]{2,0,1:T(8,128)S(1)}, u32[]{:S(2)}) copy-start(f32[16,1,192]{2,0,1:T(8,128)S(1)} %copy.43) | copy-start | bytes 36868
where the time goes:
time: 137 us
  blocking collectives  69.3 us (51%)
  waiting for transfers between devices  28.1 us (21%)
  starting transfers between devices  12.7 us (9%)
  matrix products  11.1 us (8%)
  local copies, waits for them, and re-layouts  8.15 us (6%)
  other arithmetic  4.47 us (3%)
  between operations  2.83 us (2%)
    all_gather x2, blocking collectives, extended_state(): partition = lax.all_gather(state, 'blk', axis=0, tiled=True)  52.9 us
    all_to_all x2, waiting for transfers between devices, cross_partition(): lax.all_to_all(outgoing, 'dom', split_axis=0, concat_axis=0, tiled=True)  28.1 us
    unnamed x1, blocking collectives  16.4 us
    all_to_all x2, starting transfers between devices, cross_partition(): lax.all_to_all(outgoing, 'dom', split_axis=0, concat_axis=0, tiled=True)  12.7 us
    dot_general x2, matrix products, sweep_once(): jnp.einsum('bim,bm->bi', offd, picked, preferred_element_type=jnp.float32)  10.3 us
  transfers between devices with their start and end apart: 2, of which 2 were waited for; matrix products, arithmetic and copies ran while one was open for 2% of the time, Pallas kernels for 0%

commit v1 on v0

--- a/solution.py
+++ b/solution.py
@@ -16,7 +16,9 @@
 
 
 def extended_state(state, face_index, partner_id):
-    partition = lax.all_gather(state, "blk", axis=0, tiled=True)
+    partition = jnp.concatenate(
+        lax.all_to_all(jnp.stack([state] * lax.axis_size("blk")), "blk", 0, 0), axis=0
+    )
     halo_blocks = cross_partition(partition[face_index], partner_id)
     return jnp.concatenate([partition, halo_blocks], axis=0)
 

time: 137 us -> 111 us (0.81)
  blocking collectives: 69.3 us -> 25.5 us
  starting transfers between devices: 12.7 us -> 21.2 us
  waiting for transfers between devices: 28.1 us -> 35.2 us
    all_gather x2 -> x0, blocking collectives: 52.9 us -> none  [extended_state(): partition = lax.all_gather(state, 'blk', axis=0, tiled=True)]
    all_to_all x0 -> x1, blocking collectives: none -> 10.8 us  [extended_state(): lax.all_to_all(jnp.stack([state] * lax.axis_size('blk')), 'blk', 0, 0)]
    all_to_all x0 -> x1, starting transfers between devices: none -> 8.47 us  [extended_state(): lax.all_to_all(jnp.stack([state] * lax.axis_size('blk')), 'blk', 0, 0)]
    all_to_all x0 -> x1, waiting for transfers between devices: none -> 7.05 us  [extended_state(): lax.all_to_all(jnp.stack([state] * lax.axis_size('blk')), 'blk', 0, 0)]
    unnamed x1, blocking collectives: 16.4 us -> 14.7 us
  transfers between devices with their start and end apart: 2 -> 3, of which waited for: 2 -> 3; matrix products, arithmetic and copies ran while one was open for 2% -> 3% of each run, Pallas kernels for 0% -> 0%
where the time goes in v1:
time: 111 us; the launch traced here: 110 us
  waiting for transfers between devices  35.2 us (32%)
  blocking collectives  25.5 us (23%)
  starting transfers between devices  21.2 us (19%)
  matrix products  11.1 us (10%)
  local copies, waits for them, and re-layouts  9.49 us (9%)
  other arithmetic  4.46 us (4%)
  between operations  2.83 us (3%)
    all_to_all x2, waiting for transfers between devices, cross_partition(): lax.all_to_all(outgoing, 'dom', split_axis=0, concat_axis=0, tiled=True)  28.1 us
    unnamed x1, blocking collectives  14.7 us
    all_to_all x2, starting transfers between devices, cross_partition(): lax.all_to_all(outgoing, 'dom', split_axis=0, concat_axis=0, tiled=True)  12.7 us
    all_to_all x1, blocking collectives, extended_state(): lax.all_to_all(jnp.stack([state] * lax.axis_size('blk')), 'blk', 0, 0)  10.8 us
    dot_general x2, matrix products, sweep_once(): jnp.einsum('bim,bm->bi', offd, picked, preferred_element_type=jnp.float32)  10.3 us
    all_to_all x1, starting transfers between devices, extended_state(): lax.all_to_all(jnp.stack([state] * lax.axis_size('blk')), 'blk', 0, 0)  8.47 us
    all_to_all x1, waiting for transfers between devices, extended_state(): lax.all_to_all(jnp.stack([state] * lax.axis_size('blk')), 'blk', 0, 0)  7.05 us
    mul x2, other arithmetic, cross_partition(): outgoing = onehot[:, None, None] * face_rows[None, :, :]  2.27 us
  transfers between devices with their start and end apart: 3, of which 3 were waited for; matrix products, arithmetic and copies ran while one was open for 3% of the time, Pallas kernels for 0%

profile of v1, /device:TPU:2, one launch (start us, length us, event | category | flops | bytes accessed | tf_op | source)
XLA Modules:
  0.0 109.8 jit_solution(6710811000102775525)
XLA Ops:
  0.6 1.3 %stack.4 = bf16[8,16,192]{2,1,0:T(8,128)(2,1)} broadcast(bf16[16,192]{1,0:T(8,128)(2,1)} %param.13), dimensions={1,2} | broadcast | bytes 55296 | tf_op jit(solution)/shard_map/stack | solution.py:20
  2.0 8.5 %all-to-all-start = ((bf16[8,16,192]{2,1,0:T(8,128)(2,1)}), bf16[8,16,192]{2,1,0:T(8,128)(2,1)S(1)}, u32[]{:S(2)}, u32[]{:S(2)}) async-start(bf16[8,16,192]{2,1,0:T(8,128)(2,1)} %stack.4), calls=%async_computation | async-start | bytes 131072 | tf_op jit(solution)/shard_map/all_to_all | solution.py:20
  11.1 0.7 fusion.10
  11.8 7.1 %all-to-all-done = bf16[8,16,192]{2,1,0:T(8,128)(2,1)S(1)} async-done(((bf16[8,16,192]{2,1,0:T(8,128)(2,1)}), bf16[8,16,192]{2,1,0:T(8,128)(2,1)S(1)}, u32[]{:S(2)}, u32[]{:S(2)}) %all-to-all-start) | async-done | bytes 49184 | tf_op jit(solution)/shard_map/all_to_all | solution.py:20
  18.8 0.7 gather_fusion
  19.5 0.0 copy-start.4
  19.5 0.0 copy-start.1
  19.5 1.2 %broadcast_multiply_fusion.1 = bf16[32,64,192]{2,1,0:T(8,128)(2,1)} fusion(bf16[64,192]{1,0:T(8,128)(2,1)S(1)} %gather_fusion, bf16[32]{0:T(256)(128)(2,1)S(1)} %compare_convert_fusion), kind=kLoop, calls=%fused_computation.8 | loop fusion | flops 393216 | bytes 811072 | tf_op jit(solution)/shard_map/mul | solution.py:12
  20.7 7.7 %all-to-all-start.1 = ((bf16[32,64,192]{2,1,0:T(8,128)(2,1)}), bf16[32,64,192]{2,1,0:T(8,128)(2,1)}, u32[]{:S(2)}, u32[]{:S(2)}) async-start(bf16[32,64,192]{2,1,0:T(8,128)(2,1)} %broadcast_multiply_fusion.1), calls=%async_computation.1 | async-start | bytes 2097152 | tf_op jit(solution)/shard_map/all_to_all | solution.py:13
  28.4 0.0 copy-done.4
  28.4 0.1 copy.18
  28.5 0.1 reshape.74
  29.2 0.0 copy-done.1
  29.2 0.7 copy.29
  29.9 1.3 %dynamic_slice.11 = f32[1]{0:T(128)} dynamic-slice(f32[1024]{0:T(1024)} %param.22, s32[]{:T(128)S(6)} %select_n.27), dynamic_slice_sizes={1} | dynamic-slice | bytes 12 | tf_op jit(solution)/shard_map/jit(dynamic_index_in_dim)/dynamic_slice | solution.py:48
  31.2 13.3 %all-to-all-done.1 = bf16[32,64,192]{2,1,0:T(8,128)(2,1)} async-done(((bf16[32,64,192]{2,1,0:T(8,128)(2,1)}), bf16[32,64,192]{2,1,0:T(8,128)(2,1)}, u32[]{:S(2)}, u32[]{:S(2)}) %all-to-all-start.1) | async-done | bytes 786464 | tf_op jit(solution)/shard_map/all_to_all | solution.py:13
  44.5 0.8 dynamic-slice_bitcast_fusion.1
  45.3 0.8 gather_fusion.1
  46.1 0.1 reshape.122
  46.2 0.0 copy-start.3
  46.2 5.2 %fusion.12 = f32[16,1,192]{2,1,0:T(1,128)S(1)} fusion(bf16[16,1152,1]{1,2,0:T(2,128)(2,1)S(1)} %reshape.122, bf16[16,192,1152]{2,1,0:T(8,128)(2,1)} %param.14), kind=kOutput, calls=%fused_computation.38 | convolution fusion | flops 7077888 | bytes 7127040 | tf_op jit(solution)/shard_map/bim,bm->bi/dot_general | solution.py:29
  51.4 0.0 copy-done.3
  51.4 0.7 fusion.8
  52.1 0.3 fusion.6
  52.4 10.8 %all_to_all.20 = bf16[8,16,192]{2,1,0:T(8,128)(2,1)S(1)} all-to-all(bf16[8,16,192]{2,1,0:T(8,128)(2,1)S(1)} %stack.5), channel_id=1, replica_groups=mesh['dom'=32,'blk'=8] {'blk'}, dimensions={0} | all-to-all | bytes 98304 | tf_op jit(solution)/shard_map/all_to_all | solution.py:20
  63.2 0.7 gather_fusion.2
  63.9 0.0 copy-start.2
  63.9 0.0 copy-start.7
  63.9 0.0 copy-start.5
  63.9 1.1 %broadcast_multiply_fusion = bf16[32,64,192]{2,1,0:T(8,128)(2,1)} fusion(bf16[64,192]{1,0:T(8,128)(2,1)S(1)} %gather_fusion.2, bf16[32]{0:T(256)(128)(2,1)S(1)} %compare_convert_fusion), kind=kLoop, calls=%fused_computation.7 | loop fusion | flops 393216 | bytes 811072 | tf_op jit(solution)/shard_map/mul | solution.py:12
  65.0 5.0 %all-to-all-start.3 = ((bf16[32,64,192]{2,1,0:T(8,128)(2,1)}), bf16[32,64,192]{2,1,0:T(8,128)(2,1)S(1)}, u32[]{:S(2)}, u32[]{:S(2)}) async-start(bf16[32,64,192]{2,1,0:T(8,128)(2,1)} %broadcast_multiply_fusion), calls=%async_computation.3 | async-start | bytes 2097152 | tf_op jit(solution)/shard_map/all_to_all | solution.py:13
  70.1 0.0 copy-done.2
  70.1 0.1 copy.19
  70.2 0.0 copy-done.7
  70.2 0.6 dynamic-slice
  71.4 0.0 copy-done.5
  71.5 14.8 %all-to-all-done.3 = bf16[32,64,192]{2,1,0:T(8,128)(2,1)S(1)} async-done(((bf16[32,64,192]{2,1,0:T(8,128)(2,1)}), bf16[32,64,192]{2,1,0:T(8,128)(2,1)S(1)}, u32[]{:S(2)}, u32[]{:S(2)}) %all-to-all-start.3) | async-done | bytes 786464 | tf_op jit(solution)/shard_map/all_to_all | solution.py:13
  86.3 0.8 gather_fusion.3
  87.1 0.1 reshape.124
  87.2 5.2 %fusion.13 = f32[16,1,192]{2,1,0:T(1,128)S(1)} fusion(bf16[16,1152,1]{1,2,0:T(2,128)(2,1)S(1)} %reshape.124, bf16[16,192,1152]{2,1,0:T(8,128)(2,1)} %param.14), kind=kOutput, calls=%fused_computation.39 | convolution fusion | flops 7077888 | bytes 7127040 | tf_op jit(solution)/shard_map/bim,bm->bi/dot_general | solution.py:29
  92.3 0.7 fusion.9
  93.0 0.3 fusion.4
  93.4 0.8 gather_fusion.4
  94.1 0.1 multiply_reduce_fusion
  94.2 0.0 copy-done.6
  94.2 0.2 fusion
  94.4 14.7 %all-reduce = f32[64]{0:T(128)S(1)} all-reduce(f32[64]{0:T(128)S(1)} %fusion), channel_id=2, replica_groups=mesh['dom'=32,'blk'=8] {'blk'}, use_global_device_ids=true, to_apply=%region_1.2.clone | all-reduce | flops 64 | bytes 512
  109.2 0.6 dynamic-slice.1
  (15 shorter events, 0.1 us)
Async XLA Ops:
  2.0 16.8 %all-to-all-start = ((bf16[8,16,192]{2,1,0:T(8,128)(2,1)}), bf16[8,16,192]{2,1,0:T(8,128)(2,1)S(1)}, u32[]{:S(2)}, u32[]{:S(2)}) async-start(bf16[8,16,192]{2,1,0:T(8,128)(2,1)} %stack.4), calls=%async_computation | async-start | bytes 131072 | tf_op jit(solution)/shard_map/all_to_all | solution.py:20
  19.5 8.9 %copy-start.4 = (s32[16,6]{0,1:T(8,128)S(1)}, s32[16,6]{0,1:T(8,128)}, u32[]{:S(2)}) copy-start(s32[16,6]{0,1:T(8,128)} %param.16) | copy-start | bytes 1156
  19.5 9.7 %copy-start.1 = (bf16[192,3072]{1,0:T(8,128)(2,1)S(1)}, bf16[192,3072]{1,0:T(8,128)(2,1)}, u32[]{:S(2)}) copy-start(bf16[192,3072]{1,0:T(8,128)(2,1)} %param.15) | copy-start | bytes 3538948
  20.7 23.8 %all-to-all-start.1 = ((bf16[32,64,192]{2,1,0:T(8,128)(2,1)}), bf16[32,64,192]{2,1,0:T(8,128)(2,1)}, u32[]{:S(2)}, u32[]{:S(2)}) async-start(bf16[32,64,192]{2,1,0:T(8,128)(2,1)} %broadcast_multiply_fusion.1), calls=%async_computation.1 | async-start | bytes 2097152 | tf_op jit(solution)/shard_map/all_to_all | solution.py:13
  46.2 5.2 %copy-start.3 = (bf16[16,192]{1,0:T(8,128)(2,1)S(1)}, bf16[16,192]{1,0:T(8,128)(2,1)}, u32[]{:S(2)}) copy-start(bf16[16,192]{1,0:T(8,128)(2,1)} %param.12) | copy-start | bytes 18436
  63.9 6.2 %copy-start.2 = (bf16[128,192]{0,1:T(8,128)(2,1)S(1)}, bf16[128,192]{0,1:T(8,128)(2,1)}, u32[]{:S(2)}) copy-start(bf16[128,192]{0,1:T(8,128)(2,1)} %param.21) | copy-start | bytes 147460
  63.9 6.3 %copy-start.7 = (u32[256]{0:T(256)S(1)}, u32[256]{0:T(256)}, u32[]{:S(2)}) copy-start(u32[256]{0:T(256)} %constant.35) | copy-start | bytes 3076
  63.9 7.6 %copy-start.5 = (s32[128]{0:T(128)S(1)}, s32[128]{0:T(128)}, u32[]{:S(2)}) copy-start(s32[128]{0:T(128)} %param.19) | copy-start | bytes 1540
  65.0 21.3 %all-to-all-start.3 = ((bf16[32,64,192]{2,1,0:T(8,128)(2,1)}), bf16[32,64,192]{2,1,0:T(8,128)(2,1)S(1)}, u32[]{:S(2)}, u32[]{:S(2)}) async-start(bf16[32,64,192]{2,1,0:T(8,128)(2,1)} %broadcast_multiply_fusion), calls=%async_computation.3 | async-start | bytes 2097152 | tf_op jit(solution)/shard_map/all_to_all | solution.py:13
  92.3 1.9 %copy-start.6 = (s32[128]{0:T(128)S(1)}, s32[128]{0:T(128)}, u32[]{:S(2)}) copy-start(s32[128]{0:T(128)} %param.20) | copy-start | bytes 1540
  93.4 16.4 %copy-start = (f32[16,1,192]{2,0,1:T(8,128)}, f32[16,1,192]{2,0,1:T(8,128)S(1)}, u32[]{:S(2)}) copy-start(f32[16,1,192]{2,0,1:T(8,128)S(1)} %copy.43) | copy-start | bytes 36868
